TPU v7x, 32 devices: a whole 2x2x4 slice. The times are simulated.
32 devices in a mesh: dp: 2 (over core), expert: 16 (over z, y, x).
Axes of the slice: x: 2, y: 2, z: 4, core: 2. Of those that a mesh axis runs over, the one named last changes fastest.
Arguments:
- tokens: bfloat16 [2048, 2048], P(('dp', 'expert')), may hold values from -6 to 6
- tangent: bfloat16 [2048, 2048], P(('dp', 'expert'))
- adjoint: bfloat16 [2048, 2048], P(('dp', 'expert')), may hold values from -6 to 6
- gates: float32 [2048, 8], P(('dp', 'expert')), may hold values from 0.05 to 0.5
- expert_ids: int32 [2048, 8], P(('dp', 'expert')), may hold values from 0 to 31, all different within a row; in each aligned block of 64 rows (0 to 63, 64 to 127, ...) at most 32 rows name the same one
- w_gate: bfloat16 [32, 2048, 768], P('expert'), may hold values from -0.125 to 0.125
- w_up: bfloat16 [32, 2048, 768], P('expert'), may hold values from -0.125 to 0.125
- w_down: bfloat16 [32, 768, 2048], P('expert'), may hold values from -0.21875 to 0.21875
Outputs:
- hvp: float32 [2048, 2048], P(('dp', 'expert'))
- quotient: float32 [], replicated
Inputs may be any that keep to these rules, and one draw needn't show every extreme that they name: `expert_ids`: each token names 8 different experts. Among the tokens of one device no expert is named more than 32 times, a bound that some block reaches; every expert is named somewhere.
All inputs are finite; a program needn't handle non-finite values.
Results may differ from a plain program's by a relative error of at most 0.0041.
Values may be sent and summed in bfloat16 or wider, within the bound.
No kernel may reach another device: no remote copies, remote signals or barrier semaphores. Data moves between devices by JAX's collectives and lax.ppermute only.
A program may use at most 128 MiB of HBM per device.

v0:
```python
import functools

import jax
import jax.numpy as jnp
from jax import lax
from jax.experimental import pallas as pl
from jax.experimental.pallas import tpu as pltpu
from jax.sharding import PartitionSpec as P

F32, BF16 = jnp.float32, jnp.bfloat16
NT = (((1,), (1,)), ((), ()))


def expert_kernel(shapes, part, start, *refs):
    count = len(shapes)
    pieces, (gates, w_gate, w_up, w_down) = refs[:count], refs[count : count + 4]
    outs, (both, adj, total) = refs[count + 4 : -3], refs[-3:]
    rows, width = adj.shape
    experts, _, hidden = w_gate.shape
    at = 0
    for piece, (blocks, r) in zip(pieces, shapes):
        for b in range(blocks):
            both[at : at + r] = piece[b, :r]
            both[rows + at : rows + at + r] = piece[b, r : 2 * r]
            adj[at : at + r] = piece[b, 2 * r :]
            at += r

    def parts_of(e, cols):
        gate = jnp.dot(both[...], w_gate[e, :, cols], preferred_element_type=F32)
        up = jnp.dot(both[...], w_up[e, :, cols], preferred_element_type=F32)
        back = lax.dot_general(w_down[e, cols, :], adj[...], NT, preferred_element_type=F32).T
        pre, pre_dir, lin, lin_dir = gate[:rows], gate[rows:], up[:rows], up[rows:]
        s = jax.nn.sigmoid(pre)
        first = s * (1.0 + pre * (1.0 - s))
        second = s * (1.0 - s) * (2.0 + pre * (1.0 - 2.0 * s))
        part_gate = back * (lin_dir * first + lin * second * pre_dir)
        part_up = back * first * pre_dir
        return part_gate.T.astype(BF16), part_up.T.astype(BF16)

    for e in range(experts):
        parts = [parts_of(e, slice(j, j + part)) for j in range(0, hidden, part)]
        part_gate = jnp.concatenate([p[0] for p in parts], axis=0)
        part_up = jnp.concatenate([p[1] for p in parts], axis=0)
        weight = gates[e, :, start : start + rows]
        chunk = 512 if width % 512 == 0 else width
        for c in range(0, width, chunk):
            cols = slice(c, c + chunk)
            reply = jnp.dot(w_gate[e, cols, :], part_gate, preferred_element_type=F32)
            reply += jnp.dot(w_up[e, cols, :], part_up, preferred_element_type=F32)
            term = jnp.where(weight != 0.0, weight * reply.astype(BF16).astype(F32), 0.0)
            if e > 0:
                term += total[cols, :]
            if e < experts - 1:
                total[cols, :] = term
                continue
            term = term.T
            at = 0
            for out in outs:
                blocks, r, _ = out.shape
                for b in range(blocks):
                    out[b, :, cols] = term[at : at + r].astype(out.dtype)
                    at += r


def expert_call(pieces, kinds, start, gates, w_gate, w_up, w_down):
    width = pieces[0].shape[2]
    shapes = tuple((p.shape[0], p.shape[1] // 3) for p in pieces)
    rows = sum(b * r for b, r in shapes)
    experts, _, hidden = w_gate.shape
    part = 256 if hidden % 256 == 0 else hidden
    near = pl.BlockSpec(memory_space=pltpu.VMEM)
    out_shape, at = [], 0
    for number, kind in kinds:
        group = shapes[at : at + number]
        out_shape.append(
            jax.ShapeDtypeStruct((sum(b for b, _ in group), group[0][1], width), kind)
        )
        at += number
    return pl.pallas_call(
        functools.partial(expert_kernel, shapes, part, start),
        in_specs=[near] * (len(pieces) + 4),
        out_specs=[near] * len(out_shape),
        out_shape=out_shape,
        scratch_shapes=[
            pltpu.VMEM((2 * rows, width), BF16),
            pltpu.VMEM((rows, width), BF16),
            pltpu.VMEM((width, rows), F32),
        ],
        compiler_params=pltpu.CompilerParams(vmem_limit_bytes=20 * 1024 * 1024),
        cost_estimate=pl.CostEstimate(
            flops=14 * rows * width * hidden * experts,
            bytes_accessed=8 * rows * width,
            transcendentals=rows * hidden * experts,
        ),
    )(*pieces, gates, w_gate, w_up, w_down)


def pack(ranges, *arrays):
    count, width = len(arrays), arrays[0].shape[1]

    def kernel(*refs):
        sems = refs[-1]
        copies = []
        for out, (lo, hi) in zip(refs[count:-1], ranges):
            for i, ref in enumerate(refs[:count]):
                to = out.at[0, i * (hi - lo) : (i + 1) * (hi - lo)]
                copies.append(pltpu.make_async_copy(ref.at[lo:hi], to, sems.at[len(copies)]))
                copies[-1].start()
        for copy in copies:
            copy.wait()

    return pl.pallas_call(
        kernel,
        in_specs=[pl.BlockSpec(memory_space=pl.ANY)] * count,
        out_specs=[pl.BlockSpec(memory_space=pltpu.VMEM)] * len(ranges),
        out_shape=[
            jax.ShapeDtypeStruct((1, count * (hi - lo), width), arrays[0].dtype)
            for lo, hi in ranges
        ],
        scratch_shapes=[pltpu.SemaphoreType.DMA((count * len(ranges),))],
        compiler_params=pltpu.CompilerParams(vmem_limit_bytes=4 * 1024 * 1024),
    )(*arrays)


def touch(value, *mats):
    def kernel(value_ref, *refs):
        refs[-1][...] = value_ref[...]

    near = pl.BlockSpec(memory_space=pltpu.VMEM)
    return pl.pallas_call(
        kernel,
        in_specs=[near] * (1 + len(mats)),
        out_specs=near,
        out_shape=jax.ShapeDtypeStruct(value.shape, value.dtype),
        compiler_params=pltpu.CompilerParams(vmem_limit_bytes=4 * 1024 * 1024),
    )(value, *mats)


def local(tokens, tangent, adjoint, gates, expert_ids, w_gate, w_up, w_down):
    count = lax.axis_size("expert")
    me = lax.axis_index("expert")
    ring = 4
    layer = count // ring
    high, low = me // layer, me % layer
    experts = w_gate.shape[0]
    tok_rows, _ = expert_ids.shape
    mats = (w_gate, w_up, w_down)

    def across(a, k):
        return lax.ppermute(a, "expert", [(i, i ^ k) for i in range(count)])

    def along(a, r):
        return lax.ppermute(a, "expert", [(i, (i + layer * r) % count) for i in range(count)])

    all_ids = jnp.arange(experts * count, dtype=jnp.int32)
    dense = jnp.sum(
        jnp.where(expert_ids[:, :, None] == all_ids[None, None, :], gates[:, :, None], 0.0), axis=1
    )
    dense = dense.T.reshape(count, experts, tok_rows)

    def to_owners(dense):
        return lax.all_to_all(dense, "expert", split_axis=0, concat_axis=0, tiled=True)

    def weights_of(dense, listing):
        source = ((high - jnp.arange(ring)) % ring * layer)[:, None] + (low ^ jnp.arange(layer))
        dense = jnp.take(dense, source.reshape(-1), axis=0).reshape(ring, layer, experts, tok_rows)
        parts = [dense[r, k, :, slice(*rows)] for blocks, k, rows in listing for r in blocks]
        return jnp.concatenate(parts, axis=1)[:, None, :]

    if layer == 4:
        arrays = (tokens, tangent, adjoint)
        hvp = scheduled(across, along, to_owners, weights_of, dense, arrays, mats)
    else:
        rows = (0, tok_rows)
        listing = [(range(ring), k, rows) for k in range(layer)]
        weights = weights_of(to_owners(dense), listing)
        blocks = list(pack([rows], tokens, tangent, adjoint))
        for _ in range(ring - 1):
            blocks.append(along(blocks[-1], 1))
        mine = jnp.concatenate(blocks, axis=0)
        column = 0.0
        for k in range(layer):
            piece = across(mine, k) if k else mine
            (reply,) = expert_call([piece], [(1, BF16)], k * ring * tok_rows, weights, *mats)
            column += (across(reply, k) if k else reply).astype(F32)
        hvp = column[0]
        for r in range(1, ring):
            hvp += along(column[r].astype(BF16), -r).astype(F32)

    wide = tangent.astype(F32)
    sums = jnp.stack([jnp.sum(hvp * hvp), jnp.sum(wide * wide)])
    ways = lax.axis_size("dp") * count
    sums = jnp.broadcast_to(sums[None, None, :], (ways, 1, 2))
    sums = lax.all_to_all(sums, ("dp", "expert"), split_axis=0, concat_axis=0, tiled=True)
    sums = jnp.sum(sums, axis=(0, 1))
    return hvp, sums[0] / sums[1]


def scheduled(across, along, to_owners, weights_of, dense, arrays, mats):
    bar = lambda *values: lax.optimization_barrier(values)
    join = lambda *values: jnp.concatenate(values, axis=0)
    f32 = lambda value: value.astype(F32)
    tok_rows = arrays[0].shape[0]
    rows_a, rows_b = (0, 3 * tok_rows // 4), (3 * tok_rows // 4, tok_rows)
    every = (0, 1, 2, 3)

    def spread(r):
        return [((r,), k, rows_b) for k in every]

    order = [
        [((0, 1), 1, rows_a), ((0, 1), 2, rows_a)] + spread(0),
        [((2, 3), 1, rows_a), ((2, 3), 2, rows_a)] + spread(1),
        [(every, 3, rows_a)] + spread(2),
        [(every, 0, rows_a)] + spread(3),
    ]
    sizes = [sum(len(b) * (rows[1] - rows[0]) for b, _, rows in part) for part in order]

    def call(place, pieces, kinds):
        return expert_call(pieces, kinds, sum(sizes[:place]), weights, *mats)

    (own_a,) = pack([rows_a], *arrays)
    dense, *arrays = bar(dense, *arrays)
    (own_b,) = pack([rows_b], *arrays)
    z1, x0, y0 = along(own_a, 1), across(own_a, 1), across(own_a, 2)
    bx, by, bd = across(own_b, 1), across(own_b, 2), across(own_b, 3)
    taken = to_owners(dense)
    z1, own_a, own_b = bar(z1, own_a, own_b)
    z2, x1, y1 = along(z1, 1), across(z1, 1), across(z1, 2)
    z2, x0, y0, x1, y1 = bar(z2, x0, y0, x1, y1)
    z3, d0, e1 = along(z2, 1), across(y0, 1), across(x1, 2)
    weights, _ = bar(weights_of(taken, sum(order, [])), x1)
    weights = touch(weights, *mats)
    z1, z2, z3, d0, e1, x0, y0, x1, y1, bx, by, bd, own_a, own_b, weights = bar(
        z1, z2, z3, d0, e1, x0, y0, x1, y1, bx, by, bd, own_a, own_b, weights
    )
    a_hi = join(z2, z3)
    x_hi, y_hi = across(a_hi, 1), across(a_hi, 2)
    b0 = join(own_b, bx, by, bd)
    b1 = along(b0, 1)
    p_xlo, p_ylo, p_b0 = call(0, [x0, x1, y0, y1, b0], [(2, BF16), (2, BF16), (1, F32)])
    x_hi, y_hi, a_hi, b1, p_xlo, p_ylo, p_b0, own_a, z1, d0, e1 = bar(
        x_hi, y_hi, a_hi, b1, p_xlo, p_ylo, p_b0, own_a, z1, d0, e1
    )
    d2, e3 = across(y_hi[:1], 1), across(x_hi[1:], 2)
    got_xlo, got_ylo = across(p_xlo, 1), across(p_ylo, 2)
    b2 = along(b1, 1)
    p_xhi, p_yhi, p_b1 = call(1, [x_hi, y_hi, b1], [(1, BF16), (1, BF16), (1, BF16)])
    d2, e3, b2, p_xhi, p_yhi, p_b1, a_hi, own_a, z1, d0, e1 = bar(
        d2, e3, b2, p_xhi, p_yhi, p_b1, a_hi, own_a, z1, d0, e1
    )
    got_xhi, got_yhi = across(p_xhi, 1), across(p_yhi, 2)
    b3 = along(b2, 1)
    p_d, p_b2 = call(2, [d0, e1, d2, e3, b2], [(4, BF16), (1, BF16)])
    got_xlo, got_ylo, b3, p_d, p_b1, p_b2, a_hi, own_a, z1 = bar(
        got_xlo, got_ylo, b3, p_d, p_b1, p_b2, a_hi, own_a, z1
    )
    got_d = across(p_d, 3)
    got_b1, got_b2 = along(p_b1, -1), along(p_b2, -2)
    p_a, p_b3 = call(3, [own_a, z1, a_hi, b3], [(3, F32), (1, BF16)])
    got_xhi, got_yhi, got_d, got_b1, got_b2, p_a, p_b3 = bar(
        got_xhi, got_yhi, got_d, got_b1, got_b2, p_a, p_b3
    )
    got_b3 = along(p_b3, -3)
    got_x, got_y = (got_xlo, got_xhi), (got_ylo, got_yhi)
    s = [
        p_a[r] + f32(got_x[r // 2][r % 2]) + f32(got_y[r // 2][r % 2]) + f32(got_d[r])
        for r in every
    ]
    got_s = [along(s[r].astype(BF16), -r) for r in (1, 2, 3)]
    s_b = p_b0 + f32(got_b1) + f32(got_b2) + f32(got_b3)
    got = [across(s_b[k].astype(BF16), k) for k in (1, 2, 3)]
    hvp_a = s[0] + f32(got_s[0]) + f32(got_s[1]) + f32(got_s[2])
    hvp_b = s_b[0] + f32(got[0]) + f32(got[1]) + f32(got[2])
    return join(hvp_a, hvp_b)


def solution(mesh):
    split = P(("dp", "expert"), None)
    return jax.shard_map(
        local,
        mesh=mesh,
        in_specs=(split,) * 5 + (P("expert", None, None),) * 3,
        out_specs=(split, P()),
        check_vma=False,
    )
```

profile of v0, /device:TPU:0, one launch (start us, length us, event | category | flops | bytes accessed | tf_op | source)
XLA Modules:
  0.0 183.0 jit_solution(9167998405023758067)
XLA Ops:
  4.3 3.1 %collective-permute-start = (bf16[1,144,2048]{2,1,0:T(8,128)(2,1)S(1)}, bf16[1,144,2048]{2,1,0:T(8,128)(2,1)S(1)}, u32[]{:S(2)}, u32[]{:S(2)}) collective-permute-start(bf16[1,144,2048]{2,1,0:T(8,128)(2,1)S(1)} %shard_map.95.refs_0_), channel_id=1, source_target_pairs={{0,4},{1,5},{2,6},{3,7},{4,8},{5,9},{6,10},{7,11},{8,12},{9,13},{1... | collective-permute-start | bytes 1769480 | tf_op jit(solution)/shard_map/ppermute | solution.py:153
  11.1 4.0 %all-to-all-start = ((f32[16,1,128]{2,1,0:T(1,128)}), f32[16,1,128]{2,1,0:T(1,128)S(1)}, u32[]{:S(2)}, u32[]{:S(2)}) async-start(f32[16,1,128]{2,1,0:T(1,128)} %reshape.113), calls=%async_computation | async-start | bytes 16384 | tf_op jit(solution)/shard_map/all_to_all | solution.py:162
  15.5 7.3 %collective-permute-done.refs_1_ = bf16[1,144,2048]{2,1,0:T(8,128)(2,1)S(1)} collective-permute-done((bf16[1,144,2048]{2,1,0:T(8,128)(2,1)S(1)}, bf16[1,144,2048]{2,1,0:T(8,128)(2,1)S(1)}, u32[]{:S(2)}, u32[]{:S(2)}) %collective-permute-start) | collective-permute-done | bytes 589856 | tf_op jit(solution)/shard_map/ppermute | solution.py:153
  31.2 7.9 %collective-permute-done.1 = bf16[1,144,2048]{2,1,0:T(8,128)(2,1)} collective-permute-done((bf16[1,144,2048]{2,1,0:T(8,128)(2,1)S(1)}, bf16[1,144,2048]{2,1,0:T(8,128)(2,1)}, u32[]{:S(2)}, u32[]{:S(2)}) %collective-permute-start.1) | collective-permute-done | bytes 589856 | tf_op jit(solution)/shard_map/ppermute | solution.py:153
  39.2 5.7 %collective-permute-done.5.refs_3_ = bf16[1,144,2048]{2,1,0:T(8,128)(2,1)} collective-permute-done((bf16[1,144,2048]{2,1,0:T(8,128)(2,1)S(1)}, bf16[1,144,2048]{2,1,0:T(8,128)(2,1)}, u32[]{:S(2)}, u32[]{:S(2)}) %collective-permute-start.5) | collective-permute-done | bytes 589856 | tf_op jit(solution)/shard_map/ppermute | solution.py:150
  52.9 2.8 %copy-done = bf16[2,2048,768]{2,1,0:T(8,128)(2,1)S(1)} copy-done((bf16[2,2048,768]{2,1,0:T(8,128)(2,1)S(1)}, bf16[2,2048,768]{2,1,0:T(8,128)(2,1)}, u32[]{:S(2)}) %copy-start) | copy-done | bytes 6291480
  55.6 2.8 %copy-done.2 = bf16[2,2048,768]{2,1,0:T(8,128)(2,1)S(1)} copy-done((bf16[2,2048,768]{2,1,0:T(8,128)(2,1)S(1)}, bf16[2,2048,768]{2,1,0:T(8,128)(2,1)}, u32[]{:S(2)}) %copy-start.2) | copy-done | bytes 6291480
  58.4 2.8 %copy-done.4 = bf16[2,768,2048]{2,1,0:T(8,128)(2,1)S(1)} copy-done((bf16[2,768,2048]{2,1,0:T(8,128)(2,1)S(1)}, bf16[2,768,2048]{2,1,0:T(8,128)(2,1)}, u32[]{:S(2)}) %copy-start.4) | copy-done | bytes 6291480
  62.5 1.7 constant_dynamic-update-slice_fusion.refs_2_
  65.6 1.7 constant_dynamic-update-slice_fusion.4
  67.4 1.9 %collective-permute-start.14 = (bf16[4,48,2048]{2,1,0:T(8,128)(2,1)S(1)}, bf16[4,48,2048]{2,1,0:T(8,128)(2,1)S(1)}, u32[]{:S(2)}, u32[]{:S(2)}) collective-permute-start(bf16[4,48,2048]{2,1,0:T(8,128)(2,1)S(1)} %constant_dynamic-update-slice_fusion.2.refs_4_), channel_id=1, source_target_pairs={{0,4},{1,5},{2,6},{3,7},{4,8},{5,9},{6,10},{7,11},{8,12},{9,13},{1... | collective-permute-start | bytes 2359304 | tf_op jit(solution)/shard_map/ppermute | solution.py:153
  69.2 13.7 %shard_map.98 = (bf16[2,48,2048]{2,1,0:T(8,128)(2,1)S(1)}, bf16[2,48,2048]{2,1,0:T(8,128)(2,1)S(1)}, f32[4,16,2048]{2,1,0:T(8,128)S(1)}) custom-call(bf16[1,144,2048]{2,1,0:T(8,128)(2,1)S(1)} %collective-permute-done.2.refs_0_, bf16[1,144,2048]{2,1,0:T(8,128)(2,1)} %collective-permute-done.4.refs_1_, ...), custom_call_target="tpu_custom_call" | custom-call | flops 11274289152 | bytes 4194304 | tf_op jit(solution)/shard_map/pallas_call | solution.py:79
  83.0 2.2 %collective-permute-done.14.refs_2_ = bf16[4,48,2048]{2,1,0:T(8,128)(2,1)S(1)} collective-permute-done((bf16[4,48,2048]{2,1,0:T(8,128)(2,1)S(1)}, bf16[4,48,2048]{2,1,0:T(8,128)(2,1)S(1)}, u32[]{:S(2)}, u32[]{:S(2)}) %collective-permute-start.14) | collective-permute-done | bytes 786464 | tf_op jit(solution)/shard_map/ppermute | solution.py:153
  85.2 4.1 %collective-permute-done.12.refs_0_ = bf16[2,144,2048]{2,1,0:T(8,128)(2,1)S(1)} collective-permute-done((bf16[2,144,2048]{2,1,0:T(8,128)(2,1)S(1)}, bf16[2,144,2048]{2,1,0:T(8,128)(2,1)S(1)}, u32[]{:S(2)}, u32[]{:S(2)}) %collective-permute-start.12) | collective-permute-done | bytes 1179680 | tf_op jit(solution)/shard_map/ppermute | solution.py:150
  92.7 1.7 collective-permute-start.17
  96.3 12.5 %shard_map.99 = (bf16[2,48,2048]{2,1,0:T(8,128)(2,1)S(1)}, bf16[2,48,2048]{2,1,0:T(8,128)(2,1)S(1)}, bf16[4,16,2048]{2,1,0:T(8,128)(2,1)S(1)}) custom-call(bf16[2,144,2048]{2,1,0:T(8,128)(2,1)S(1)} %collective-permute-done.12.refs_0_, bf16[2,144,2048]{2,1,0:T(8,128)(2,1)S(1)} %collective-permute-done.13.refs_1_, ...), custom_call_target="tpu_custom_call" | custom-call | flops 11274289152 | bytes 4194304 | tf_op jit(solution)/shard_map/pallas_call | solution.py:79
  113.3 13.5 %shard_map.100 = (bf16[4,48,2048]{2,1,0:T(8,128)(2,1)S(1)}, bf16[4,16,2048]{2,1,0:T(8,128)(2,1)S(1)}) custom-call(bf16[1,144,2048]{2,1,0:T(8,128)(2,1)} %collective-permute-done.7.refs_0_, bf16[1,144,2048]{2,1,0:T(8,128)(2,1)S(1)} %collective-permute-done.8.refs_1_, bf16[1,144,2048]{2,1,0:T(8,128)(2,1)S(1)} %collective-permute-done.15.refs_2_, ...), custom_call_target="tpu_custom_call" | custom-call | flops 11274289152 | bytes 4194304 | tf_op jit(solution)/shard_map/pallas_call | solution.py:79
  128.3 3.4 %collective-permute-start.24 = (bf16[4,16,2048]{2,1,0:T(8,128)(2,1)S(1)}, bf16[4,16,2048]{2,1,0:T(8,128)(2,1)S(1)}, u32[]{:S(2)}, u32[]{:S(2)}) collective-permute-start(bf16[4,16,2048]{2,1,0:T(8,128)(2,1)S(1)} %get-tuple-element.136), channel_id=1, source_target_pairs={{0,12},{1,13},{2,14},{3,15},{4,0},{5,1},{6,2},{7,3},{8,4},{9,5},{1... | collective-permute-start | bytes 786440 | tf_op jit(solution)/shard_map/ppermute | solution.py:153
  131.7 12.5 %shard_map.101 = (f32[4,48,2048]{2,1,0:T(8,128)S(1)}, bf16[4,16,2048]{2,1,0:T(8,128)(2,1)S(1)}) custom-call(bf16[1,144,2048]{2,1,0:T(8,128)(2,1)S(1)} %shard_map.95.refs_0_, bf16[1,144,2048]{2,1,0:T(8,128)(2,1)S(1)} %collective-permute-done.refs_1_, bf16[2,144,2048]{2,1,0:T(8,128)(2,1)S(1)} %constant_dynamic-update-slice_fusion.refs_2_, ...), custom_call_target="tpu_custom_call" | custom-call | flops 11274289152 | bytes 4194304 | tf_op jit(solution)/shard_map/pallas_call | solution.py:79
  144.2 8.2 %collective-permute-done.25 = bf16[4,16,2048]{2,1,0:T(8,128)(2,1)S(1)} collective-permute-done((bf16[4,16,2048]{2,1,0:T(8,128)(2,1)S(1)}, bf16[4,16,2048]{2,1,0:T(8,128)(2,1)S(1)}, u32[]{:S(2)}, u32[]{:S(2)}) %collective-permute-start.25) | collective-permute-done | bytes 262176 | tf_op jit(solution)/shard_map/ppermute | solution.py:153
  152.7 3.9 %collective-permute-start.26 = (bf16[48,2048]{1,0:T(8,128)(2,1)S(1)}, bf16[48,2048]{1,0:T(8,128)(2,1)S(1)}, u32[]{:S(2)}, u32[]{:S(2)}) collective-permute-start(bf16[48,2048]{1,0:T(8,128)(2,1)S(1)} %get-tuple-element.160), channel_id=1, source_target_pairs={{0,12},{1,13},{2,14},{3,15},{4,0},{5,1},{6,2},{7,3},{8,4},{9,5},{1... | collective-permute-start | bytes 589832 | tf_op jit(solution)/shard_map/ppermute | solution.py:153
  157.2 3.5 %collective-permute-done.29 = bf16[4,16,2048]{2,1,0:T(8,128)(2,1)S(1)} collective-permute-done((bf16[4,16,2048]{2,1,0:T(8,128)(2,1)S(1)}, bf16[4,16,2048]{2,1,0:T(8,128)(2,1)S(1)}, u32[]{:S(2)}, u32[]{:S(2)}) %collective-permute-start.29) | collective-permute-done | bytes 262176 | tf_op jit(solution)/shard_map/ppermute | solution.py:153
  164.4 3.0 %collective-permute-done.27 = bf16[48,2048]{1,0:T(8,128)(2,1)S(1)} collective-permute-done((bf16[48,2048]{1,0:T(8,128)(2,1)S(1)}, bf16[48,2048]{1,0:T(8,128)(2,1)S(1)}, u32[]{:S(2)}, u32[]{:S(2)}) %collective-permute-start.27) | collective-permute-done | bytes 196640 | tf_op jit(solution)/shard_map/ppermute | solution.py:153
  170.9 8.8 %all_to_all.10 = f32[32,1,2]{2,1,0:T(1,128)S(1)} all-to-all(f32[32,1,2]{2,1,0:T(1,128)S(1)} %broadcast_in_dim.41), channel_id=1, replica_groups=mesh['dp'=2,'expert'=16] {'dp','expert'}, dimensions={0} | all-to-all | bytes 512 | tf_op jit(solution)/shard_map/all_to_all | solution.py:194
  (116 shorter events, 46.9 us)
Async XLA Ops:
  4.3 18.6 %collective-permute-start = (bf16[1,144,2048]{2,1,0:T(8,128)(2,1)S(1)}, bf16[1,144,2048]{2,1,0:T(8,128)(2,1)S(1)}, u32[]{:S(2)}, u32[]{:S(2)}) collective-permute-start(bf16[1,144,2048]{2,1,0:T(8,128)(2,1)S(1)} %shard_map.95.refs_0_), channel_id=1, source_target_pairs={{0,4},{1,5},{2,6},{3,7},{4,8},{5,9},{6,10},{7,11},{8,12},{9,13},{1... | collective-permute-start | bytes 1769480 | tf_op jit(solution)/shard_map/ppermute | solution.py:153
  7.4 21.8 %collective-permute-start.2 = (bf16[1,144,2048]{2,1,0:T(8,128)(2,1)S(1)}, bf16[1,144,2048]{2,1,0:T(8,128)(2,1)S(1)}, u32[]{:S(2)}, u32[]{:S(2)}) collective-permute-start(bf16[1,144,2048]{2,1,0:T(8,128)(2,1)S(1)} %shard_map.95.refs_0_), channel_id=1, source_target_pairs={{0,1},{1,0},{2,3},{3,2},{4,5},{5,4},{6,7},{7,6},{8,9},{9,8},{10,11... | collective-permute-start | bytes 1769480 | tf_op jit(solution)/shard_map/ppermute | solution.py:150
  8.9 20.9 %collective-permute-start.3 = (bf16[1,144,2048]{2,1,0:T(8,128)(2,1)S(1)}, bf16[1,144,2048]{2,1,0:T(8,128)(2,1)S(1)}, u32[]{:S(2)}, u32[]{:S(2)}) collective-permute-start(bf16[1,144,2048]{2,1,0:T(8,128)(2,1)S(1)} %shard_map.95.refs_0_), channel_id=1, source_target_pairs={{0,2},{1,3},{2,0},{3,1},{4,6},{5,7},{6,4},{7,5},{8,10},{9,11},{10,... | collective-permute-start | bytes 1769480 | tf_op jit(solution)/shard_map/ppermute | solution.py:150
  11.1 16.2 %all-to-all-start = ((f32[16,1,128]{2,1,0:T(1,128)}), f32[16,1,128]{2,1,0:T(1,128)S(1)}, u32[]{:S(2)}, u32[]{:S(2)}) async-start(f32[16,1,128]{2,1,0:T(1,128)} %reshape.113), calls=%async_computation | async-start | bytes 16384 | tf_op jit(solution)/shard_map/all_to_all | solution.py:162
  22.9 16.3 %collective-permute-start.1 = (bf16[1,144,2048]{2,1,0:T(8,128)(2,1)S(1)}, bf16[1,144,2048]{2,1,0:T(8,128)(2,1)}, u32[]{:S(2)}, u32[]{:S(2)}) collective-permute-start(bf16[1,144,2048]{2,1,0:T(8,128)(2,1)S(1)} %collective-permute-done.refs_1_), channel_id=1, source_target_pairs={{0,4},{1,5},{2,6},{3,7},{4,8},{5,9},{6,10},{7,11},{8,12},{9,13},{1... | collective-permute-start | bytes 1769480 | tf_op jit(solution)/shard_map/ppermute | solution.py:153
  22.9 16.4 %collective-permute-start.4 = (bf16[1,144,2048]{2,1,0:T(8,128)(2,1)S(1)}, bf16[1,144,2048]{2,1,0:T(8,128)(2,1)}, u32[]{:S(2)}, u32[]{:S(2)}) collective-permute-start(bf16[1,144,2048]{2,1,0:T(8,128)(2,1)S(1)} %collective-permute-done.refs_1_), channel_id=1, source_target_pairs={{0,1},{1,0},{2,3},{3,2},{4,5},{5,4},{6,7},{7,6},{8,9},{9,8},{10,11... | collective-permute-start | bytes 1769480 | tf_op jit(solution)/shard_map/ppermute | solution.py:150
  24.4 20.6 %collective-permute-start.5 = (bf16[1,144,2048]{2,1,0:T(8,128)(2,1)S(1)}, bf16[1,144,2048]{2,1,0:T(8,128)(2,1)}, u32[]{:S(2)}, u32[]{:S(2)}) collective-permute-start(bf16[1,144,2048]{2,1,0:T(8,128)(2,1)S(1)} %collective-permute-done.refs_1_), channel_id=1, source_target_pairs={{0,2},{1,3},{2,0},{3,1},{4,6},{5,7},{6,4},{7,5},{8,10},{9,11},{10,... | collective-permute-start | bytes 1769480 | tf_op jit(solution)/shard_map/ppermute | solution.py:150
  29.2 20.5 %collective-permute-start.10 = (bf16[1,48,2048]{2,1,0:T(8,128)(2,1)S(1)}, bf16[1,48,2048]{2,1,0:T(8,128)(2,1)S(1)}, u32[]{:S(2)}, u32[]{:S(2)}) collective-permute-start(bf16[1,48,2048]{2,1,0:T(8,128)(2,1)S(1)} %shard_map.96), channel_id=1, source_target_pairs={{0,2},{1,3},{2,0},{3,1},{4,6},{5,7},{6,4},{7,5},{8,10},{9,11},{10,... | collective-permute-start | bytes 589832 | tf_op jit(solution)/shard_map/ppermute | solution.py:150
  29.8 31.5 %collective-permute-start.11 = (bf16[1,48,2048]{2,1,0:T(8,128)(2,1)S(1)}, bf16[1,48,2048]{2,1,0:T(8,128)(2,1)S(1)}, u32[]{:S(2)}, u32[]{:S(2)}) collective-permute-start(bf16[1,48,2048]{2,1,0:T(8,128)(2,1)S(1)} %shard_map.96), channel_id=1, source_target_pairs={{0,3},{1,2},{2,1},{3,0},{4,7},{5,6},{6,5},{7,4},{8,11},{9,10},{10,... | collective-permute-start | bytes 589832 | tf_op jit(solution)/shard_map/ppermute | solution.py:150
  44.9 16.3 %collective-permute-start.8 = (bf16[1,144,2048]{2,1,0:T(8,128)(2,1)}, bf16[1,144,2048]{2,1,0:T(8,128)(2,1)S(1)}, u32[]{:S(2)}, u32[]{:S(2)}) collective-permute-start(bf16[1,144,2048]{2,1,0:T(8,128)(2,1)} %collective-permute-done.4.refs_1_), channel_id=1, source_target_pairs={{0,2},{1,3},{2,0},{3,1},{4,6},{5,7},{6,4},{7,5},{8,10},{9,11},{10,... | collective-permute-start | bytes 1769480 | tf_op jit(solution)/shard_map/ppermute | solution.py:150
  64.2 25.1 %collective-permute-start.12 = (bf16[2,144,2048]{2,1,0:T(8,128)(2,1)S(1)}, bf16[2,144,2048]{2,1,0:T(8,128)(2,1)S(1)}, u32[]{:S(2)}, u32[]{:S(2)}) collective-permute-start(bf16[2,144,2048]{2,1,0:T(8,128)(2,1)S(1)} %constant_dynamic-update-slice_fusion.refs_2_), channel_id=1, source_target_pairs={{0,1},{1,0},{2,3},{3,2},{4,5},{5,4},{6,7},{7,6},{8,9},{9,8},{10,11... | collective-permute-start | bytes 3538952 | tf_op jit(solution)/shard_map/ppermute | solution.py:150
  64.8 24.9 %collective-permute-start.13 = (bf16[2,144,2048]{2,1,0:T(8,128)(2,1)S(1)}, bf16[2,144,2048]{2,1,0:T(8,128)(2,1)S(1)}, u32[]{:S(2)}, u32[]{:S(2)}) collective-permute-start(bf16[2,144,2048]{2,1,0:T(8,128)(2,1)S(1)} %constant_dynamic-update-slice_fusion.refs_2_), channel_id=1, source_target_pairs={{0,2},{1,3},{2,0},{3,1},{4,6},{5,7},{6,4},{7,5},{8,10},{9,11},{10,... | collective-permute-start | bytes 3538952 | tf_op jit(solution)/shard_map/ppermute | solution.py:150
  67.4 17.8 %collective-permute-start.14 = (bf16[4,48,2048]{2,1,0:T(8,128)(2,1)S(1)}, bf16[4,48,2048]{2,1,0:T(8,128)(2,1)S(1)}, u32[]{:S(2)}, u32[]{:S(2)}) collective-permute-start(bf16[4,48,2048]{2,1,0:T(8,128)(2,1)S(1)} %constant_dynamic-update-slice_fusion.2.refs_4_), channel_id=1, source_target_pairs={{0,4},{1,5},{2,6},{3,7},{4,8},{5,9},{6,10},{7,11},{8,12},{9,13},{1... | collective-permute-start | bytes 2359304 | tf_op jit(solution)/shard_map/ppermute | solution.py:153
  89.7 19.0 %collective-permute-start.15 = (bf16[1,144,2048]{2,1,0:T(8,128)(2,1)S(1)}, bf16[1,144,2048]{2,1,0:T(8,128)(2,1)S(1)}, u32[]{:S(2)}, u32[]{:S(2)}) collective-permute-start(bf16[1,144,2048]{2,1,0:T(8,128)(2,1)S(1)} %slice.203), channel_id=1, source_target_pairs={{0,1},{1,0},{2,3},{3,2},{4,5},{5,4},{6,7},{7,6},{8,9},{9,8},{10,11... | collective-permute-start | bytes 1769480 | tf_op jit(solution)/shard_map/ppermute | solution.py:150
  91.1 17.6 %collective-permute-start.16 = (bf16[1,144,2048]{2,1,0:T(8,128)(2,1)S(1)}, bf16[1,144,2048]{2,1,0:T(8,128)(2,1)S(1)}, u32[]{:S(2)}, u32[]{:S(2)}) collective-permute-start(bf16[1,144,2048]{2,1,0:T(8,128)(2,1)S(1)} %slice.204), channel_id=1, source_target_pairs={{0,2},{1,3},{2,0},{3,1},{4,6},{5,7},{6,4},{7,5},{8,10},{9,11},{10,... | collective-permute-start | bytes 1769480 | tf_op jit(solution)/shard_map/ppermute | solution.py:150
  92.7 17.7 %collective-permute-start.17 = (bf16[4,48,2048]{2,1,0:T(8,128)(2,1)S(1)}, bf16[4,48,2048]{2,1,0:T(8,128)(2,1)S(1)}, u32[]{:S(2)}, u32[]{:S(2)}) collective-permute-start(bf16[4,48,2048]{2,1,0:T(8,128)(2,1)S(1)} %collective-permute-done.14.refs_2_), channel_id=1, source_target_pairs={{0,4},{1,5},{2,6},{3,7},{4,8},{5,9},{6,10},{7,11},{8,12},{9,13},{1... | collective-permute-start | bytes 2359304 | tf_op jit(solution)/shard_map/ppermute | solution.py:153
  94.3 32.5 %collective-permute-start.20 = (bf16[2,48,2048]{2,1,0:T(8,128)(2,1)S(1)}, bf16[2,48,2048]{2,1,0:T(8,128)(2,1)S(1)}, u32[]{:S(2)}, u32[]{:S(2)}) collective-permute-start(bf16[2,48,2048]{2,1,0:T(8,128)(2,1)S(1)} %get-tuple-element.122), channel_id=1, source_target_pairs={{0,1},{1,0},{2,3},{3,2},{4,5},{5,4},{6,7},{7,6},{8,9},{9,8},{10,11... | collective-permute-start | bytes 1179656 | tf_op jit(solution)/shard_map/ppermute | solution.py:150
  94.7 32.1 %collective-permute-start.21 = (bf16[2,48,2048]{2,1,0:T(8,128)(2,1)S(1)}, bf16[2,48,2048]{2,1,0:T(8,128)(2,1)S(1)}, u32[]{:S(2)}, u32[]{:S(2)}) collective-permute-start(bf16[2,48,2048]{2,1,0:T(8,128)(2,1)S(1)} %get-tuple-element.123), channel_id=1, source_target_pairs={{0,2},{1,3},{2,0},{3,1},{4,6},{5,7},{6,4},{7,5},{8,10},{9,11},{10,... | collective-permute-start | bytes 1179656 | tf_op jit(solution)/shard_map/ppermute | solution.py:150
  110.3 17.2 %collective-permute-start.22 = (bf16[4,48,2048]{2,1,0:T(8,128)(2,1)S(1)}, bf16[4,48,2048]{2,1,0:T(8,128)(2,1)S(1)}, u32[]{:S(2)}, u32[]{:S(2)}) collective-permute-start(bf16[4,48,2048]{2,1,0:T(8,128)(2,1)S(1)} %collective-permute-done.17.refs_4_), channel_id=1, source_target_pairs={{0,4},{1,5},{2,6},{3,7},{4,8},{5,9},{6,10},{7,11},{8,12},{9,13},{1... | collective-permute-start | bytes 2359304 | tf_op jit(solution)/shard_map/ppermute | solution.py:153
  111.2 33.0 %collective-permute-start.18 = (bf16[2,48,2048]{2,1,0:T(8,128)(2,1)S(1)}, bf16[2,48,2048]{2,1,0:T(8,128)(2,1)S(1)}, u32[]{:S(2)}, u32[]{:S(2)}) collective-permute-start(bf16[2,48,2048]{2,1,0:T(8,128)(2,1)S(1)} %get-tuple-element.120), channel_id=1, source_target_pairs={{0,1},{1,0},{2,3},{3,2},{4,5},{5,4},{6,7},{7,6},{8,9},{9,8},{10,11... | collective-permute-start | bytes 1179656 | tf_op jit(solution)/shard_map/ppermute | solution.py:150
  112.1 32.1 %collective-permute-start.19 = (bf16[2,48,2048]{2,1,0:T(8,128)(2,1)S(1)}, bf16[2,48,2048]{2,1,0:T(8,128)(2,1)S(1)}, u32[]{:S(2)}, u32[]{:S(2)}) collective-permute-start(bf16[2,48,2048]{2,1,0:T(8,128)(2,1)S(1)} %get-tuple-element.121), channel_id=1, source_target_pairs={{0,2},{1,3},{2,0},{3,1},{4,6},{5,7},{6,4},{7,5},{8,10},{9,11},{10,... | collective-permute-start | bytes 1179656 | tf_op jit(solution)/shard_map/ppermute | solution.py:150
  127.5 24.9 %collective-permute-start.23 = (bf16[4,48,2048]{2,1,0:T(8,128)(2,1)S(1)}, bf16[4,48,2048]{2,1,0:T(8,128)(2,1)S(1)}, u32[]{:S(2)}, u32[]{:S(2)}) collective-permute-start(bf16[4,48,2048]{2,1,0:T(8,128)(2,1)S(1)} %get-tuple-element.135), channel_id=1, source_target_pairs={{0,3},{1,2},{2,1},{3,0},{4,7},{5,6},{6,5},{7,4},{8,11},{9,10},{10,... | collective-permute-start | bytes 2359304 | tf_op jit(solution)/shard_map/ppermute | solution.py:150
  128.3 15.9 %collective-permute-start.24 = (bf16[4,16,2048]{2,1,0:T(8,128)(2,1)S(1)}, bf16[4,16,2048]{2,1,0:T(8,128)(2,1)S(1)}, u32[]{:S(2)}, u32[]{:S(2)}) collective-permute-start(bf16[4,16,2048]{2,1,0:T(8,128)(2,1)S(1)} %get-tuple-element.136), channel_id=1, source_target_pairs={{0,12},{1,13},{2,14},{3,15},{4,0},{5,1},{6,2},{7,3},{8,4},{9,5},{1... | collective-permute-start | bytes 786440 | tf_op jit(solution)/shard_map/ppermute | solution.py:153
  131.7 20.7 %collective-permute-start.25 = (bf16[4,16,2048]{2,1,0:T(8,128)(2,1)S(1)}, bf16[4,16,2048]{2,1,0:T(8,128)(2,1)S(1)}, u32[]{:S(2)}, u32[]{:S(2)}) collective-permute-start(bf16[4,16,2048]{2,1,0:T(8,128)(2,1)S(1)} %get-tuple-element.137), channel_id=1, source_target_pairs={{0,8},{1,9},{2,10},{3,11},{4,12},{5,13},{6,14},{7,15},{8,0},{9,1},... | collective-permute-start | bytes 786440 | tf_op jit(solution)/shard_map/ppermute | solution.py:153
  (24 other events, 182.1 us)
where the time goes:
time: 186 us; the launch traced here: 183 us
  Pallas kernels  53.3 us (29%)
  waiting for transfers between devices  46.8 us (25%)
  starting transfers between devices  43.4 us (23%)
  local copies, waits for them, and re-layouts  20.8 us (11%)
  blocking collectives  8.82 us (5%)
  other arithmetic  6.29 us (3%)
  between operations  3.66 us (2%)
    pallas_call x4, Pallas kernels, expert_call(): pl.pallas_call(functools.partial(expert_kernel, shapes, part, start), in_...  52.2 us
    ppermute x12, waiting for transfers between devices, along(): lax.ppermute(a, 'expert', [(i, (i + layer * r) % count) for i in range(co...  35.9 us
    ppermute x21, starting transfers between devices, across(): return lax.ppermute(a, 'expert', [(i, i ^ k) for i in range(count)])  22.7 us
    ppermute x12, starting transfers between devices, along(): lax.ppermute(a, 'expert', [(i, (i + layer * r) % count) for i in range(co...  16.7 us
    unnamed x34, local copies, waits for them, and re-layouts  15 us
    ppermute x21, waiting for transfers between devices, across(): return lax.ppermute(a, 'expert', [(i, i ^ k) for i in range(count)])  10.9 us
    all_to_all x1, blocking collectives, local(): lax.all_to_all(sums, ('dp', 'expert'), split_axis=0, concat_axis=0, tiled...  8.82 us
    all_to_all x1, starting transfers between devices, to_owners(): lax.all_to_all(dense, 'expert', split_axis=0, concat_axis=0, tiled=True)  3.97 us
  transfers between devices with their start and end apart: 34, of which 14 were waited for; matrix products, arithmetic and copies ran while one was open for 5% of the time, Pallas kernels for 29%

commit v1 on v0

--- a/solution.py
+++ b/solution.py
@@ -86,7 +86,7 @@
             pltpu.VMEM((rows, width), BF16),
             pltpu.VMEM((width, rows), F32),
         ],
-        compiler_params=pltpu.CompilerParams(vmem_limit_bytes=20 * 1024 * 1024),
+        compiler_params=pltpu.CompilerParams(vmem_limit_bytes=22 * 1024 * 1024),
         cost_estimate=pl.CostEstimate(
             flops=14 * rows * width * hidden * experts,
             bytes_accessed=8 * rows * width,
@@ -208,9 +208,9 @@
         return [((r,), k, rows_b) for k in every]
 
     order = [
-        [((0, 1), 1, rows_a), ((0, 1), 2, rows_a)] + spread(0),
+        [((0, 1), 1, rows_a), ((0, 1), 2, rows_a), ((0, 1), 3, rows_a)] + spread(0),
         [((2, 3), 1, rows_a), ((2, 3), 2, rows_a)] + spread(1),
-        [(every, 3, rows_a)] + spread(2),
+        [((2, 3), 3, rows_a)] + spread(2),
         [(every, 0, rows_a)] + spread(3),
     ]
     sizes = [sum(len(b) * (rows[1] - rows[0]) for b, _, rows in part) for part in order]
@@ -233,37 +233,39 @@
     z1, z2, z3, d0, e1, x0, y0, x1, y1, bx, by, bd, own_a, own_b, weights = bar(
         z1, z2, z3, d0, e1, x0, y0, x1, y1, bx, by, bd, own_a, own_b, weights
     )
-    a_hi = join(z2, z3)
-    x_hi, y_hi = across(a_hi, 1), across(a_hi, 2)
+    x2, y2, x3, y3 = across(z2, 1), across(z2, 2), across(z3, 1), across(z3, 2)
     b0 = join(own_b, bx, by, bd)
     b1 = along(b0, 1)
-    p_xlo, p_ylo, p_b0 = call(0, [x0, x1, y0, y1, b0], [(2, BF16), (2, BF16), (1, F32)])
-    x_hi, y_hi, a_hi, b1, p_xlo, p_ylo, p_b0, own_a, z1, d0, e1 = bar(
-        x_hi, y_hi, a_hi, b1, p_xlo, p_ylo, p_b0, own_a, z1, d0, e1
-    )
-    d2, e3 = across(y_hi[:1], 1), across(x_hi[1:], 2)
+    p_xlo, p_ylo, p_d01, p_b0 = call(
+        0, [x0, x1, y0, y1, d0, e1, b0], [(2, BF16), (2, BF16), (2, BF16), (1, F32)]
+    )
+    x2, y2, x3, y3, b1, p_xlo, p_ylo, p_d01, p_b0, own_a, z1, z2, z3 = bar(
+        x2, y2, x3, y3, b1, p_xlo, p_ylo, p_d01, p_b0, own_a, z1, z2, z3
+    )
+    d2, e3 = across(y2, 1), across(x3, 2)
     got_xlo, got_ylo = across(p_xlo, 1), across(p_ylo, 2)
     b2 = along(b1, 1)
-    p_xhi, p_yhi, p_b1 = call(1, [x_hi, y_hi, b1], [(1, BF16), (1, BF16), (1, BF16)])
-    d2, e3, b2, p_xhi, p_yhi, p_b1, a_hi, own_a, z1, d0, e1 = bar(
-        d2, e3, b2, p_xhi, p_yhi, p_b1, a_hi, own_a, z1, d0, e1
-    )
+    p_xhi, p_yhi, p_b1 = call(1, [x2, x3, y2, y3, b1], [(2, BF16), (2, BF16), (1, BF16)])
+    d2, e3, b2, p_xhi, p_yhi, p_b1, p_d01, own_a, z1, z2, z3 = bar(
+        d2, e3, b2, p_xhi, p_yhi, p_b1, p_d01, own_a, z1, z2, z3
+    )
+    got_d01 = across(p_d01, 3)
     got_xhi, got_yhi = across(p_xhi, 1), across(p_yhi, 2)
     b3 = along(b2, 1)
-    p_d, p_b2 = call(2, [d0, e1, d2, e3, b2], [(4, BF16), (1, BF16)])
-    got_xlo, got_ylo, b3, p_d, p_b1, p_b2, a_hi, own_a, z1 = bar(
-        got_xlo, got_ylo, b3, p_d, p_b1, p_b2, a_hi, own_a, z1
-    )
-    got_d = across(p_d, 3)
+    p_d23, p_b2 = call(2, [d2, e3, b2], [(2, BF16), (1, BF16)])
+    got_xlo, got_ylo, b3, p_d23, p_b1, p_b2, own_a, z1, z2, z3 = bar(
+        got_xlo, got_ylo, b3, p_d23, p_b1, p_b2, own_a, z1, z2, z3
+    )
+    got_d23 = across(p_d23, 3)
     got_b1, got_b2 = along(p_b1, -1), along(p_b2, -2)
-    p_a, p_b3 = call(3, [own_a, z1, a_hi, b3], [(3, F32), (1, BF16)])
-    got_xhi, got_yhi, got_d, got_b1, got_b2, p_a, p_b3 = bar(
-        got_xhi, got_yhi, got_d, got_b1, got_b2, p_a, p_b3
+    p_a, p_b3 = call(3, [own_a, z1, z2, z3, b3], [(4, F32), (1, BF16)])
+    got_xhi, got_yhi, got_d01, got_d23, got_b1, got_b2, p_a, p_b3 = bar(
+        got_xhi, got_yhi, got_d01, got_d23, got_b1, got_b2, p_a, p_b3
     )
     got_b3 = along(p_b3, -3)
-    got_x, got_y = (got_xlo, got_xhi), (got_ylo, got_yhi)
+    got_x, got_y, got_d = (got_xlo, got_xhi), (got_ylo, got_yhi), (got_d01, got_d23)
     s = [
-        p_a[r] + f32(got_x[r // 2][r % 2]) + f32(got_y[r // 2][r % 2]) + f32(got_d[r])
+        p_a[r] + f32(got_x[r // 2][r % 2]) + f32(got_y[r // 2][r % 2]) + f32(got_d[r // 2][r % 2])
         for r in every
     ]
     got_s = [along(s[r].astype(BF16), -r) for r in (1, 2, 3)]

time: 186 us -> 185 us (level)
  waiting for transfers between devices: 46.8 us -> 30.9 us
  starting transfers between devices: 43.4 us -> 50 us
  Pallas kernels: 53.3 us -> 58.7 us
    ppermute x12, waiting for transfers between devices: 35.9 us -> 24.5 us  [along(): lax.ppermute(a, 'expert', [(i, (i + layer * r) % count) for i in range(co...]
    pallas_call x4, Pallas kernels: 52.2 us -> 57.7 us  [expert_call(): pl.pallas_call(functools.partial(expert_kernel, shapes, part, start), in_...]
    ppermute x21 -> x24, waiting for transfers between devices: 10.9 us -> 6.46 us  [across(): return lax.ppermute(a, 'expert', [(i, i ^ k) for i in range(count)])]
    ppermute x21 -> x24, starting transfers between devices: 22.7 us -> 26.3 us  [across(): return lax.ppermute(a, 'expert', [(i, i ^ k) for i in range(count)])]
    ppermute x12, starting transfers between devices: 16.7 us -> 19.8 us  [along(): lax.ppermute(a, 'expert', [(i, (i + layer * r) % count) for i in range(co...]
    unnamed x34 -> x31, local copies, waits for them, and re-layouts: 15 us -> 16.5 us
  transfers between devices with their start and end apart: 34 -> 37, of which waited for: 14 -> 9; matrix products, arithmetic and copies ran while one was open for 5% -> 6% of each run, Pallas kernels for 29% -> 32%
where the time goes in v1:
time: 185 us; the launch traced here: 181 us
  Pallas kernels  58.7 us (32%)
  starting transfers between devices  50 us (27%)
  waiting for transfers between devices  30.9 us (17%)
  local copies, waits for them, and re-layouts  20.7 us (11%)
  blocking collectives  10.1 us (5%)
  other arithmetic  7.27 us (4%)
  between operations  3.57 us (2%)
    pallas_call x4, Pallas kernels, expert_call(): pl.pallas_call(functools.partial(expert_kernel, shapes, part, start), in_...  57.7 us
    ppermute x24, starting transfers between devices, across(): return lax.ppermute(a, 'expert', [(i, i ^ k) for i in range(count)])  26.3 us
    ppermute x12, waiting for transfers between devices, along(): lax.ppermute(a, 'expert', [(i, (i + layer * r) % count) for i in range(co...  24.5 us
    ppermute x12, starting transfers between devices, along(): lax.ppermute(a, 'expert', [(i, (i + layer * r) % count) for i in range(co...  19.8 us
    unnamed x31, local copies, waits for them, and re-layouts  16.5 us
    all_to_all x1, blocking collectives, local(): lax.all_to_all(sums, ('dp', 'expert'), split_axis=0, concat_axis=0, tiled...  10.1 us
    ppermute x24, waiting for transfers between devices, across(): return lax.ppermute(a, 'expert', [(i, i ^ k) for i in range(count)])  6.46 us
    all_to_all x1, starting transfers between devices, to_owners(): lax.all_to_all(dense, 'expert', split_axis=0, concat_axis=0, tiled=True)  3.97 us
  transfers between devices with their start and end apart: 37, of which 9 were waited for; matrix products, arithmetic and copies ran while one was open for 6% of the time, Pallas kernels for 32%

profile of v1, /device:TPU:0, one launch (start us, length us, event | category | flops | bytes accessed | tf_op | source)
XLA Modules:
  0.0 181.3 jit_solution(16675757314543713461)
XLA Ops:
  4.2 3.1 %collective-permute-start = (bf16[1,144,2048]{2,1,0:T(8,128)(2,1)S(1)}, bf16[1,144,2048]{2,1,0:T(8,128)(2,1)S(1)}, u32[]{:S(2)}, u32[]{:S(2)}) collective-permute-start(bf16[1,144,2048]{2,1,0:T(8,128)(2,1)S(1)} %shard_map.95.refs_0_), channel_id=1, source_target_pairs={{0,4},{1,5},{2,6},{3,7},{4,8},{5,9},{6,10},{7,11},{8,12},{9,13},{1... | collective-permute-start | bytes 1769480 | tf_op jit(solution)/shard_map/ppermute | solution.py:153
  11.8 4.0 %all-to-all-start = ((f32[16,1,128]{2,1,0:T(1,128)}), f32[16,1,128]{2,1,0:T(1,128)S(1)}, u32[]{:S(2)}, u32[]{:S(2)}) async-start(f32[16,1,128]{2,1,0:T(1,128)} %reshape.113), calls=%async_computation | async-start | bytes 16384 | tf_op jit(solution)/shard_map/all_to_all | solution.py:162
  18.9 3.9 %collective-permute-done.refs_1_ = bf16[1,144,2048]{2,1,0:T(8,128)(2,1)S(1)} collective-permute-done((bf16[1,144,2048]{2,1,0:T(8,128)(2,1)S(1)}, bf16[1,144,2048]{2,1,0:T(8,128)(2,1)S(1)}, u32[]{:S(2)}, u32[]{:S(2)}) %collective-permute-start) | collective-permute-done | bytes 589856 | tf_op jit(solution)/shard_map/ppermute | solution.py:153
  30.6 8.4 %collective-permute-done.1.refs_2_ = bf16[1,144,2048]{2,1,0:T(8,128)(2,1)S(1)} collective-permute-done((bf16[1,144,2048]{2,1,0:T(8,128)(2,1)S(1)}, bf16[1,144,2048]{2,1,0:T(8,128)(2,1)S(1)}, u32[]{:S(2)}, u32[]{:S(2)}) %collective-permute-start.1) | collective-permute-done | bytes 589856 | tf_op jit(solution)/shard_map/ppermute | solution.py:153
  39.2 5.7 %collective-permute-done.5.refs_3_ = bf16[1,144,2048]{2,1,0:T(8,128)(2,1)} collective-permute-done((bf16[1,144,2048]{2,1,0:T(8,128)(2,1)S(1)}, bf16[1,144,2048]{2,1,0:T(8,128)(2,1)}, u32[]{:S(2)}, u32[]{:S(2)}) %collective-permute-start.5) | collective-permute-done | bytes 589856 | tf_op jit(solution)/shard_map/ppermute | solution.py:150
  52.9 2.8 %copy-done = bf16[2,2048,768]{2,1,0:T(8,128)(2,1)S(1)} copy-done((bf16[2,2048,768]{2,1,0:T(8,128)(2,1)S(1)}, bf16[2,2048,768]{2,1,0:T(8,128)(2,1)}, u32[]{:S(2)}) %copy-start) | copy-done | bytes 6291480
  55.7 2.8 %copy-done.2 = bf16[2,2048,768]{2,1,0:T(8,128)(2,1)S(1)} copy-done((bf16[2,2048,768]{2,1,0:T(8,128)(2,1)S(1)}, bf16[2,2048,768]{2,1,0:T(8,128)(2,1)}, u32[]{:S(2)}) %copy-start.2) | copy-done | bytes 6291480
  58.4 2.8 %copy-done.4 = bf16[2,768,2048]{2,1,0:T(8,128)(2,1)S(1)} copy-done((bf16[2,768,2048]{2,1,0:T(8,128)(2,1)S(1)}, bf16[2,768,2048]{2,1,0:T(8,128)(2,1)}, u32[]{:S(2)}) %copy-start.4) | copy-done | bytes 6291480
  65.4 1.7 constant_dynamic-update-slice_fusion.2
  67.2 1.8 collective-permute-start.16
  69.0 21.1 %shard_map.98 = (bf16[2,48,2048]{2,1,0:T(8,128)(2,1)S(1)}, bf16[2,48,2048]{2,1,0:T(8,128)(2,1)S(1)}, bf16[2,48,2048]{2,1,0:T(8,128)(2,1)S(1)}, f32[4,16,2048]{2,1,0:T(8,128)S(1)}) custom-call(bf16[1,144,2048]{2,1,0:T(8,128)(2,1)S(1)} %collective-permute-done.2.refs_0_, bf16[1,144,2048]{2,1,0:T(8,128)(2,1)} %collective-permute-done.4.refs_1_, ...), custom_call_target="tpu_custom_call" | custom-call | flops 15502147584 | bytes 5767168 | tf_op jit(solution)/shard_map/pallas_call | solution.py:79
  90.1 2.2 %collective-permute-start.19 = (bf16[4,48,2048]{2,1,0:T(8,128)(2,1)S(1)}, bf16[4,48,2048]{2,1,0:T(8,128)(2,1)S(1)}, u32[]{:S(2)}, u32[]{:S(2)}) collective-permute-start(bf16[4,48,2048]{2,1,0:T(8,128)(2,1)S(1)} %collective-permute-done.16.refs_4_), channel_id=1, source_target_pairs={{0,4},{1,5},{2,6},{3,7},{4,8},{5,9},{6,10},{7,11},{8,12},{9,13},{1... | collective-permute-start | bytes 2359304 | tf_op jit(solution)/shard_map/ppermute | solution.py:153
  93.3 12.9 %shard_map.99 = (bf16[2,48,2048]{2,1,0:T(8,128)(2,1)S(1)}, bf16[2,48,2048]{2,1,0:T(8,128)(2,1)S(1)}, bf16[4,16,2048]{2,1,0:T(8,128)(2,1)S(1)}) custom-call(bf16[1,144,2048]{2,1,0:T(8,128)(2,1)S(1)} %collective-permute-done.12.refs_0_, bf16[1,144,2048]{2,1,0:T(8,128)(2,1)S(1)} %collective-permute-done.14.refs_1_, ...), custom_call_target="tpu_custom_call" | custom-call | flops 11274289152 | bytes 4194304 | tf_op jit(solution)/shard_map/pallas_call | solution.py:79
  106.2 2.0 %collective-permute-start.25 = (bf16[4,48,2048]{2,1,0:T(8,128)(2,1)S(1)}, bf16[4,48,2048]{2,1,0:T(8,128)(2,1)S(1)}, u32[]{:S(2)}, u32[]{:S(2)}) collective-permute-start(bf16[4,48,2048]{2,1,0:T(8,128)(2,1)S(1)} %collective-permute-done.19.refs_2_), channel_id=1, source_target_pairs={{0,4},{1,5},{2,6},{3,7},{4,8},{5,9},{6,10},{7,11},{8,12},{9,13},{1... | collective-permute-start | bytes 2359304 | tf_op jit(solution)/shard_map/ppermute | solution.py:153
  113.1 10.3 %shard_map.100 = (bf16[2,48,2048]{2,1,0:T(8,128)(2,1)S(1)}, bf16[4,16,2048]{2,1,0:T(8,128)(2,1)S(1)}) custom-call(bf16[1,144,2048]{2,1,0:T(8,128)(2,1)S(1)} %collective-permute-done.17.refs_0_, bf16[1,144,2048]{2,1,0:T(8,128)(2,1)S(1)} %collective-permute-done.18.refs_1_, bf16[4,48,2048]{2,1,0:T(8,128)(2,1)S(1)} %collective-permute-done.19.refs_2_, ...), custom_call_target="tpu_custom_call" | custom-call | flops 7046430720 | bytes 2621440 | tf_op jit(solution)/shard_map/pallas_call | solution.py:79
  124.6 1.7 collective-permute-start.26
  126.3 2.5 %collective-permute-start.27 = (bf16[4,16,2048]{2,1,0:T(8,128)(2,1)S(1)}, bf16[4,16,2048]{2,1,0:T(8,128)(2,1)S(1)}, u32[]{:S(2)}, u32[]{:S(2)}) collective-permute-start(bf16[4,16,2048]{2,1,0:T(8,128)(2,1)S(1)} %get-tuple-element.144), channel_id=1, source_target_pairs={{0,12},{1,13},{2,14},{3,15},{4,0},{5,1},{6,2},{7,3},{8,4},{9,5},{1... | collective-permute-start | bytes 786440 | tf_op jit(solution)/shard_map/ppermute | solution.py:153
  128.8 2.5 %collective-permute-start.28 = (bf16[4,16,2048]{2,1,0:T(8,128)(2,1)S(1)}, bf16[4,16,2048]{2,1,0:T(8,128)(2,1)S(1)}, u32[]{:S(2)}, u32[]{:S(2)}) collective-permute-start(bf16[4,16,2048]{2,1,0:T(8,128)(2,1)S(1)} %get-tuple-element.145), channel_id=1, source_target_pairs={{0,8},{1,9},{2,10},{3,11},{4,12},{5,13},{6,14},{7,15},{8,0},{9,1},... | collective-permute-start | bytes 786440 | tf_op jit(solution)/shard_map/ppermute | solution.py:153
  131.3 13.5 %shard_map.101 = (f32[4,48,2048]{2,1,0:T(8,128)S(1)}, bf16[4,16,2048]{2,1,0:T(8,128)(2,1)S(1)}) custom-call(bf16[1,144,2048]{2,1,0:T(8,128)(2,1)S(1)} %shard_map.95.refs_0_, bf16[1,144,2048]{2,1,0:T(8,128)(2,1)S(1)} %collective-permute-done.refs_1_, bf16[1,144,2048]{2,1,0:T(8,128)(2,1)S(1)} %collective-permute-done.1.refs_2_, ...), custom_call_target="tpu_custom_call" | custom-call | flops 11274289152 | bytes 4194304 | tf_op jit(solution)/shard_map/pallas_call | solution.py:79
  144.9 4.5 %collective-permute-done.28 = bf16[4,16,2048]{2,1,0:T(8,128)(2,1)S(1)} collective-permute-done((bf16[4,16,2048]{2,1,0:T(8,128)(2,1)S(1)}, bf16[4,16,2048]{2,1,0:T(8,128)(2,1)S(1)}, u32[]{:S(2)}, u32[]{:S(2)}) %collective-permute-start.28) | collective-permute-done | bytes 262176 | tf_op jit(solution)/shard_map/ppermute | solution.py:153
  149.8 3.9 %collective-permute-start.29 = (bf16[48,2048]{1,0:T(8,128)(2,1)S(1)}, bf16[48,2048]{1,0:T(8,128)(2,1)S(1)}, u32[]{:S(2)}, u32[]{:S(2)}) collective-permute-start(bf16[48,2048]{1,0:T(8,128)(2,1)S(1)} %get-tuple-element.170), channel_id=1, source_target_pairs={{0,12},{1,13},{2,14},{3,15},{4,0},{5,1},{6,2},{7,3},{8,4},{9,5},{1... | collective-permute-start | bytes 589832 | tf_op jit(solution)/shard_map/ppermute | solution.py:153
  154.3 3.4 %collective-permute-done.32 = bf16[4,16,2048]{2,1,0:T(8,128)(2,1)S(1)} collective-permute-done((bf16[4,16,2048]{2,1,0:T(8,128)(2,1)S(1)}, bf16[4,16,2048]{2,1,0:T(8,128)(2,1)S(1)}, u32[]{:S(2)}, u32[]{:S(2)}) %collective-permute-start.32) | collective-permute-done | bytes 262176 | tf_op jit(solution)/shard_map/ppermute | solution.py:153
  161.4 3.0 %collective-permute-done.30 = bf16[48,2048]{1,0:T(8,128)(2,1)S(1)} collective-permute-done((bf16[48,2048]{1,0:T(8,128)(2,1)S(1)}, bf16[48,2048]{1,0:T(8,128)(2,1)S(1)}, u32[]{:S(2)}, u32[]{:S(2)}) %collective-permute-start.30) | collective-permute-done | bytes 196640 | tf_op jit(solution)/shard_map/ppermute | solution.py:153
  168.0 10.1 %all_to_all.10 = f32[32,1,2]{2,1,0:T(1,128)S(1)} all-to-all(f32[32,1,2]{2,1,0:T(1,128)S(1)} %broadcast_in_dim.41), channel_id=1, replica_groups=mesh['dp'=2,'expert'=16] {'dp','expert'}, dimensions={0} | all-to-all | bytes 512 | tf_op jit(solution)/shard_map/all_to_all | solution.py:194
  (116 shorter events, 47.4 us)
Async XLA Ops:
  4.2 18.6 %collective-permute-start = (bf16[1,144,2048]{2,1,0:T(8,128)(2,1)S(1)}, bf16[1,144,2048]{2,1,0:T(8,128)(2,1)S(1)}, u32[]{:S(2)}, u32[]{:S(2)}) collective-permute-start(bf16[1,144,2048]{2,1,0:T(8,128)(2,1)S(1)} %shard_map.95.refs_0_), channel_id=1, source_target_pairs={{0,4},{1,5},{2,6},{3,7},{4,8},{5,9},{6,10},{7,11},{8,12},{9,13},{1... | collective-permute-start | bytes 1769480 | tf_op jit(solution)/shard_map/ppermute | solution.py:153
  7.3 21.2 %collective-permute-start.2 = (bf16[1,144,2048]{2,1,0:T(8,128)(2,1)S(1)}, bf16[1,144,2048]{2,1,0:T(8,128)(2,1)S(1)}, u32[]{:S(2)}, u32[]{:S(2)}) collective-permute-start(bf16[1,144,2048]{2,1,0:T(8,128)(2,1)S(1)} %shard_map.95.refs_0_), channel_id=1, source_target_pairs={{0,1},{1,0},{2,3},{3,2},{4,5},{5,4},{6,7},{7,6},{8,9},{9,8},{10,11... | collective-permute-start | bytes 1769480 | tf_op jit(solution)/shard_map/ppermute | solution.py:150
  8.8 20.3 %collective-permute-start.3 = (bf16[1,144,2048]{2,1,0:T(8,128)(2,1)S(1)}, bf16[1,144,2048]{2,1,0:T(8,128)(2,1)S(1)}, u32[]{:S(2)}, u32[]{:S(2)}) collective-permute-start(bf16[1,144,2048]{2,1,0:T(8,128)(2,1)S(1)} %shard_map.95.refs_0_), channel_id=1, source_target_pairs={{0,2},{1,3},{2,0},{3,1},{4,6},{5,7},{6,4},{7,5},{8,10},{9,11},{10,... | collective-permute-start | bytes 1769480 | tf_op jit(solution)/shard_map/ppermute | solution.py:150
  11.8 14.9 %all-to-all-start = ((f32[16,1,128]{2,1,0:T(1,128)}), f32[16,1,128]{2,1,0:T(1,128)S(1)}, u32[]{:S(2)}, u32[]{:S(2)}) async-start(f32[16,1,128]{2,1,0:T(1,128)} %reshape.113), calls=%async_computation | async-start | bytes 16384 | tf_op jit(solution)/shard_map/all_to_all | solution.py:162
  22.8 16.2 %collective-permute-start.1 = (bf16[1,144,2048]{2,1,0:T(8,128)(2,1)S(1)}, bf16[1,144,2048]{2,1,0:T(8,128)(2,1)S(1)}, u32[]{:S(2)}, u32[]{:S(2)}) collective-permute-start(bf16[1,144,2048]{2,1,0:T(8,128)(2,1)S(1)} %collective-permute-done.refs_1_), channel_id=1, source_target_pairs={{0,4},{1,5},{2,6},{3,7},{4,8},{5,9},{6,10},{7,11},{8,12},{9,13},{1... | collective-permute-start | bytes 1769480 | tf_op jit(solution)/shard_map/ppermute | solution.py:153
  22.8 16.4 %collective-permute-start.4 = (bf16[1,144,2048]{2,1,0:T(8,128)(2,1)S(1)}, bf16[1,144,2048]{2,1,0:T(8,128)(2,1)}, u32[]{:S(2)}, u32[]{:S(2)}) collective-permute-start(bf16[1,144,2048]{2,1,0:T(8,128)(2,1)S(1)} %collective-permute-done.refs_1_), channel_id=1, source_target_pairs={{0,1},{1,0},{2,3},{3,2},{4,5},{5,4},{6,7},{7,6},{8,9},{9,8},{10,11... | collective-permute-start | bytes 1769480 | tf_op jit(solution)/shard_map/ppermute | solution.py:150
  24.3 20.6 %collective-permute-start.5 = (bf16[1,144,2048]{2,1,0:T(8,128)(2,1)S(1)}, bf16[1,144,2048]{2,1,0:T(8,128)(2,1)}, u32[]{:S(2)}, u32[]{:S(2)}) collective-permute-start(bf16[1,144,2048]{2,1,0:T(8,128)(2,1)S(1)} %collective-permute-done.refs_1_), channel_id=1, source_target_pairs={{0,2},{1,3},{2,0},{3,1},{4,6},{5,7},{6,4},{7,5},{8,10},{9,11},{10,... | collective-permute-start | bytes 1769480 | tf_op jit(solution)/shard_map/ppermute | solution.py:150
  28.5 21.2 %collective-permute-start.10 = (bf16[1,48,2048]{2,1,0:T(8,128)(2,1)S(1)}, bf16[1,48,2048]{2,1,0:T(8,128)(2,1)S(1)}, u32[]{:S(2)}, u32[]{:S(2)}) collective-permute-start(bf16[1,48,2048]{2,1,0:T(8,128)(2,1)S(1)} %shard_map.96), channel_id=1, source_target_pairs={{0,2},{1,3},{2,0},{3,1},{4,6},{5,7},{6,4},{7,5},{8,10},{9,11},{10,... | collective-permute-start | bytes 589832 | tf_op jit(solution)/shard_map/ppermute | solution.py:150
  29.1 32.1 %collective-permute-start.11 = (bf16[1,48,2048]{2,1,0:T(8,128)(2,1)S(1)}, bf16[1,48,2048]{2,1,0:T(8,128)(2,1)S(1)}, u32[]{:S(2)}, u32[]{:S(2)}) collective-permute-start(bf16[1,48,2048]{2,1,0:T(8,128)(2,1)S(1)} %shard_map.96), channel_id=1, source_target_pairs={{0,3},{1,2},{2,1},{3,0},{4,7},{5,6},{6,5},{7,4},{8,11},{9,10},{10,... | collective-permute-start | bytes 589832 | tf_op jit(solution)/shard_map/ppermute | solution.py:150
  44.9 16.4 %collective-permute-start.8 = (bf16[1,144,2048]{2,1,0:T(8,128)(2,1)}, bf16[1,144,2048]{2,1,0:T(8,128)(2,1)}, u32[]{:S(2)}, u32[]{:S(2)}) collective-permute-start(bf16[1,144,2048]{2,1,0:T(8,128)(2,1)} %collective-permute-done.4.refs_1_), channel_id=1, source_target_pairs={{0,2},{1,3},{2,0},{3,1},{4,6},{5,7},{6,4},{7,5},{8,10},{9,11},{10,... | collective-permute-start | bytes 1769480 | tf_op jit(solution)/shard_map/ppermute | solution.py:150
  61.3 28.7 %collective-permute-start.12 = (bf16[1,144,2048]{2,1,0:T(8,128)(2,1)S(1)}, bf16[1,144,2048]{2,1,0:T(8,128)(2,1)S(1)}, u32[]{:S(2)}, u32[]{:S(2)}) collective-permute-start(bf16[1,144,2048]{2,1,0:T(8,128)(2,1)S(1)} %collective-permute-done.1.refs_2_), channel_id=1, source_target_pairs={{0,1},{1,0},{2,3},{3,2},{4,5},{5,4},{6,7},{7,6},{8,9},{9,8},{10,11... | collective-permute-start | bytes 1769480 | tf_op jit(solution)/shard_map/ppermute | solution.py:150
  61.9 28.2 %collective-permute-start.13 = (bf16[1,144,2048]{2,1,0:T(8,128)(2,1)S(1)}, bf16[1,144,2048]{2,1,0:T(8,128)(2,1)S(1)}, u32[]{:S(2)}, u32[]{:S(2)}) collective-permute-start(bf16[1,144,2048]{2,1,0:T(8,128)(2,1)S(1)} %collective-permute-done.1.refs_2_), channel_id=1, source_target_pairs={{0,2},{1,3},{2,0},{3,1},{4,6},{5,7},{6,4},{7,5},{8,10},{9,11},{10,... | collective-permute-start | bytes 1769480 | tf_op jit(solution)/shard_map/ppermute | solution.py:150
  62.6 27.4 %collective-permute-start.14 = (bf16[1,144,2048]{2,1,0:T(8,128)(2,1)}, bf16[1,144,2048]{2,1,0:T(8,128)(2,1)S(1)}, u32[]{:S(2)}, u32[]{:S(2)}) collective-permute-start(bf16[1,144,2048]{2,1,0:T(8,128)(2,1)} %collective-permute-done.6.refs_3_), channel_id=1, source_target_pairs={{0,1},{1,0},{2,3},{3,2},{4,5},{5,4},{6,7},{7,6},{8,9},{9,8},{10,11... | collective-permute-start | bytes 1769480 | tf_op jit(solution)/shard_map/ppermute | solution.py:150
  63.9 26.2 %collective-permute-start.15 = (bf16[1,144,2048]{2,1,0:T(8,128)(2,1)}, bf16[1,144,2048]{2,1,0:T(8,128)(2,1)S(1)}, u32[]{:S(2)}, u32[]{:S(2)}) collective-permute-start(bf16[1,144,2048]{2,1,0:T(8,128)(2,1)} %collective-permute-done.6.refs_3_), channel_id=1, source_target_pairs={{0,2},{1,3},{2,0},{3,1},{4,6},{5,7},{6,4},{7,5},{8,10},{9,11},{10,... | collective-permute-start | bytes 1769480 | tf_op jit(solution)/shard_map/ppermute | solution.py:150
  67.2 22.9 %collective-permute-start.16 = (bf16[4,48,2048]{2,1,0:T(8,128)(2,1)S(1)}, bf16[4,48,2048]{2,1,0:T(8,128)(2,1)S(1)}, u32[]{:S(2)}, u32[]{:S(2)}) collective-permute-start(bf16[4,48,2048]{2,1,0:T(8,128)(2,1)S(1)} %constant_dynamic-update-slice_fusion.refs_6_), channel_id=1, source_target_pairs={{0,4},{1,5},{2,6},{3,7},{4,8},{5,9},{6,10},{7,11},{8,12},{9,13},{1... | collective-permute-start | bytes 2359304 | tf_op jit(solution)/shard_map/ppermute | solution.py:153
  90.1 16.1 %collective-permute-start.19 = (bf16[4,48,2048]{2,1,0:T(8,128)(2,1)S(1)}, bf16[4,48,2048]{2,1,0:T(8,128)(2,1)S(1)}, u32[]{:S(2)}, u32[]{:S(2)}) collective-permute-start(bf16[4,48,2048]{2,1,0:T(8,128)(2,1)S(1)} %collective-permute-done.16.refs_4_), channel_id=1, source_target_pairs={{0,4},{1,5},{2,6},{3,7},{4,8},{5,9},{6,10},{7,11},{8,12},{9,13},{1... | collective-permute-start | bytes 2359304 | tf_op jit(solution)/shard_map/ppermute | solution.py:153
  106.2 18.4 %collective-permute-start.25 = (bf16[4,48,2048]{2,1,0:T(8,128)(2,1)S(1)}, bf16[4,48,2048]{2,1,0:T(8,128)(2,1)S(1)}, u32[]{:S(2)}, u32[]{:S(2)}) collective-permute-start(bf16[4,48,2048]{2,1,0:T(8,128)(2,1)S(1)} %collective-permute-done.19.refs_2_), channel_id=1, source_target_pairs={{0,4},{1,5},{2,6},{3,7},{4,8},{5,9},{6,10},{7,11},{8,12},{9,13},{1... | collective-permute-start | bytes 2359304 | tf_op jit(solution)/shard_map/ppermute | solution.py:153
  109.6 15.1 %collective-permute-start.24 = (bf16[2,48,2048]{2,1,0:T(8,128)(2,1)S(1)}, bf16[2,48,2048]{2,1,0:T(8,128)(2,1)S(1)}, u32[]{:S(2)}, u32[]{:S(2)}) collective-permute-start(bf16[2,48,2048]{2,1,0:T(8,128)(2,1)S(1)} %get-tuple-element.132), channel_id=1, source_target_pairs={{0,2},{1,3},{2,0},{3,1},{4,6},{5,7},{6,4},{7,5},{8,10},{9,11},{10,... | collective-permute-start | bytes 1179656 | tf_op jit(solution)/shard_map/ppermute | solution.py:150
  110.8 18.0 %collective-permute-start.20 = (bf16[2,48,2048]{2,1,0:T(8,128)(2,1)S(1)}, bf16[2,48,2048]{2,1,0:T(8,128)(2,1)S(1)}, u32[]{:S(2)}, u32[]{:S(2)}) collective-permute-start(bf16[2,48,2048]{2,1,0:T(8,128)(2,1)S(1)} %get-tuple-element.128), channel_id=1, source_target_pairs={{0,1},{1,0},{2,3},{3,2},{4,5},{5,4},{6,7},{7,6},{8,9},{9,8},{10,11... | collective-permute-start | bytes 1179656 | tf_op jit(solution)/shard_map/ppermute | solution.py:150
  111.5 33.3 %collective-permute-start.21 = (bf16[2,48,2048]{2,1,0:T(8,128)(2,1)S(1)}, bf16[2,48,2048]{2,1,0:T(8,128)(2,1)S(1)}, u32[]{:S(2)}, u32[]{:S(2)}) collective-permute-start(bf16[2,48,2048]{2,1,0:T(8,128)(2,1)S(1)} %get-tuple-element.129), channel_id=1, source_target_pairs={{0,2},{1,3},{2,0},{3,1},{4,6},{5,7},{6,4},{7,5},{8,10},{9,11},{10,... | collective-permute-start | bytes 1179656 | tf_op jit(solution)/shard_map/ppermute | solution.py:150
  123.3 21.5 %collective-permute-start.22 = (bf16[2,48,2048]{2,1,0:T(8,128)(2,1)S(1)}, bf16[2,48,2048]{2,1,0:T(8,128)(2,1)S(1)}, u32[]{:S(2)}, u32[]{:S(2)}) collective-permute-start(bf16[2,48,2048]{2,1,0:T(8,128)(2,1)S(1)} %get-tuple-element.130), channel_id=1, source_target_pairs={{0,3},{1,2},{2,1},{3,0},{4,7},{5,6},{6,5},{7,4},{8,11},{9,10},{10,... | collective-permute-start | bytes 1179656 | tf_op jit(solution)/shard_map/ppermute | solution.py:150
  124.6 24.8 %collective-permute-start.26 = (bf16[2,48,2048]{2,1,0:T(8,128)(2,1)S(1)}, bf16[2,48,2048]{2,1,0:T(8,128)(2,1)S(1)}, u32[]{:S(2)}, u32[]{:S(2)}) collective-permute-start(bf16[2,48,2048]{2,1,0:T(8,128)(2,1)S(1)} %get-tuple-element.143), channel_id=1, source_target_pairs={{0,3},{1,2},{2,1},{3,0},{4,7},{5,6},{6,5},{7,4},{8,11},{9,10},{10,... | collective-permute-start | bytes 1179656 | tf_op jit(solution)/shard_map/ppermute | solution.py:150
  126.3 18.5 %collective-permute-start.27 = (bf16[4,16,2048]{2,1,0:T(8,128)(2,1)S(1)}, bf16[4,16,2048]{2,1,0:T(8,128)(2,1)S(1)}, u32[]{:S(2)}, u32[]{:S(2)}) collective-permute-start(bf16[4,16,2048]{2,1,0:T(8,128)(2,1)S(1)} %get-tuple-element.144), channel_id=1, source_target_pairs={{0,12},{1,13},{2,14},{3,15},{4,0},{5,1},{6,2},{7,3},{8,4},{9,5},{1... | collective-permute-start | bytes 786440 | tf_op jit(solution)/shard_map/ppermute | solution.py:153
  128.8 20.6 %collective-permute-start.28 = (bf16[4,16,2048]{2,1,0:T(8,128)(2,1)S(1)}, bf16[4,16,2048]{2,1,0:T(8,128)(2,1)S(1)}, u32[]{:S(2)}, u32[]{:S(2)}) collective-permute-start(bf16[4,16,2048]{2,1,0:T(8,128)(2,1)S(1)} %get-tuple-element.145), channel_id=1, source_target_pairs={{0,8},{1,9},{2,10},{3,11},{4,12},{5,13},{6,14},{7,15},{8,0},{9,1},... | collective-permute-start | bytes 786440 | tf_op jit(solution)/shard_map/ppermute | solution.py:153
  (26 other events, 195.4 us)
